TPU v7x, 256 devices: a whole 4x4x8 slice. The times are simulated.
256 devices in a mesh: dp: 64 (over x, z, core), mp: 4 (over y).
Axes of the slice: x: 4, y: 4, z: 8, core: 2. Of those that a mesh axis runs over, the one named last changes fastest.
Arguments:
- gradient: bfloat16 [128, 1024, 1024], P('dp', 'mp'), may hold values from -3 to 3
- left_codes: bfloat16 [128, 1024, 1024], P('dp', 'mp'), may hold values from -1 to 1
- left_scales: bfloat16 [128, 1024], P('dp', 'mp'), may hold values from 0.5 to 5
- right_codes: bfloat16 [128, 1024, 1024], P('dp', 'mp'), may hold values from -1 to 1
- right_scales: bfloat16 [128, 1024], P('dp', 'mp'), may hold values from 0.5 to 5
- left_root_codes: bfloat16 [128, 1024, 1024], P('dp', 'mp'), may hold values from -0.1 to 1, as said below
- left_root_scales: bfloat16 [128, 1024], P('dp', 'mp'), may hold values from 0.5 to 2
- right_root_codes: bfloat16 [128, 1024, 1024], P('dp', 'mp'), may hold values from -0.1 to 1, as said below
- right_root_scales: bfloat16 [128, 1024], P('dp', 'mp'), may hold values from 0.5 to 2
- owner_plan: int32 [128], replicated, may hold values from 0 to 127, as said below
Outputs:
- new_left_codes: bfloat16 [128, 1024, 1024], P('dp', 'mp')
- new_left_scales: bfloat16 [128, 1024], P('dp', 'mp')
- new_right_codes: bfloat16 [128, 1024, 1024], P('dp', 'mp')
- new_right_scales: bfloat16 [128, 1024], P('dp', 'mp')
- update: bfloat16 [128, 1024, 1024], P('dp', 'mp')
Inputs may be any that keep to these rules, and one draw needn't show every extreme that they name: `left_root_codes`: each row i has one entry on the diagonal between 0.6 and 1 and small entries elsewhere. `right_root_codes`: each row i has one entry on the diagonal between 0.6 and 1 and small entries elsewhere. `owner_plan`: A permutation of the 128 slots; slot s lies on device s // 2 of dp. Exactly 12 blocks get a slot on another device; from each device at most one block leaves and at most one arrives, and an arriving block takes the slot that the device's leaving block frees; every other block keeps its slot.
All inputs are finite; a program needn't handle non-finite values. Where the computation divides by a largest or mean magnitude, that divisor is 1e-20 or more.
Results may differ from a plain program's by a relative error of at most 0.009.
Values may be sent and summed in bfloat16 or wider, within the bound.
A program may use at most 64 MiB of HBM per device.

v0:
```python
import math
import jax
import jax.numpy as jnp
from jax import lax
from jax.sharding import PartitionSpec as P

DECAY = 0.95
EPSILON = 1e-06


def side_by_side(arrays, axis, dim, along):
    widths = [math.prod(a.shape[along:]) for a in arrays]
    both = jnp.concatenate(
        [a.reshape(*a.shape[:along], w) for a, w in zip(arrays, widths)], axis=along
    )
    result = lax.all_gather(both, axis, axis=dim, tiled=True)
    tiles = jnp.split(result, [sum(widths[:k]) for k in range(1, len(widths))], axis=along)
    return tuple(
        (b.reshape(*result.shape[:along], *a.shape[along:]) for a, b in zip(arrays, tiles))
    )


def in_one_piece(arrays, axis, split_dim, concat_dim, along):
    columns = [a.reshape(*a.shape[:along], -1) for a in arrays]
    both = jnp.concatenate(columns, axis=along)
    result, at, done = (
        lax.all_to_all(both, axis, split_axis=split_dim, concat_axis=concat_dim, tiled=True),
        0,
        [],
    )
    for a, column in zip(arrays, columns):
        slab = result[..., at : at + column.shape[along]]
        done.append(slab.reshape(*slab.shape[:along], *a.shape[along:]))
        at += column.shape[along]
    return tuple(done)


def dequantize(codes, scales):
    return codes.astype(jnp.float32) * scales.astype(jnp.float32)[..., None]


def requantize(matrix):
    scales = (jnp.max(jnp.abs(matrix), axis=-1) + EPSILON).astype(jnp.bfloat16)
    codes = (matrix / scales.astype(jnp.float32)[..., None]).astype(jnp.bfloat16)
    return (codes, scales)


def refresh(
    gradient,
    left_codes,
    left_scales,
    right_codes,
    right_scales,
    left_root_codes,
    left_root_scales,
    right_root_codes,
    right_root_scales,
):
    gathered = lax.all_gather(gradient, "mp", axis=1, tiled=True)
    height = gradient.shape[1]
    offset = lax.axis_index("mp") * height
    left_new = DECAY * dequantize(left_codes, left_scales) + jnp.einsum(
        "sik,sjk->sij", gradient, gathered, preferred_element_type=jnp.float32
    )
    columns = lax.dynamic_slice_in_dim(gathered, offset, height, 2)
    right_new = DECAY * dequantize(right_codes, right_scales) + jnp.einsum(
        "sji,sjk->sik", columns, gathered, preferred_element_type=jnp.float32
    )
    left_root = dequantize(left_root_codes, left_root_scales).astype(jnp.bfloat16)
    lifted = jnp.einsum(
        "sik,skj->sij", left_root, gathered, preferred_element_type=jnp.float32
    ).astype(jnp.bfloat16)
    code_piece, scale_piece = side_by_side((right_root_codes, right_root_scales), "mp", 1, 2)
    root_piece = dequantize(code_piece, scale_piece).astype(jnp.bfloat16)
    direction = jnp.einsum("sik,skj->sij", lifted, root_piece, preferred_element_type=jnp.float32)
    grad_square = jnp.sum(jnp.square(gradient.astype(jnp.float32)), axis=(1, 2))
    dir_square = jnp.sum(jnp.square(direction), axis=(1, 2))
    grad_total, dir_total = lax.psum((grad_square, dir_square), "mp")
    scaling = jnp.sqrt(grad_total + EPSILON) / jnp.sqrt(dir_total + EPSILON)
    update = (direction * scaling[:, None, None]).astype(jnp.bfloat16)
    left_out, left_scale = requantize(left_new)
    right_out, right_scale = requantize(right_new)
    return (update, left_out, left_scale, right_out, right_scale)


def routing(owner_plan, slot_count):
    owners = lax.axis_size("dp")
    myself = lax.axis_index("dp")
    blocks = jnp.arange(owner_plan.shape[0], dtype=jnp.int32)
    anchors = blocks // slot_count
    targets = owner_plan // slot_count
    moving = anchors != targets
    leaving = moving & (anchors == myself)
    vacancy = jnp.sum(jnp.where(leaving, blocks % slot_count, 0))
    present = jnp.any(leaving)
    device_ids = jnp.arange(owners, dtype=jnp.int32)
    forward = jnp.sum(
        jnp.where(moving[:, None] & (targets[:, None] == device_ids[None, :]), anchors[:, None], 0),
        axis=0,
    )
    backward = jnp.sum(
        jnp.where(moving[:, None] & (anchors[:, None] == device_ids[None, :]), targets[:, None], 0),
        axis=0,
    )
    retain = present & (jnp.arange(slot_count, dtype=jnp.int32) == vacancy)
    return (forward[:, None], backward[:, None], vacancy, retain)


def outgoing(values, vacancy):
    return lax.dynamic_slice_in_dim(values, vacancy, 1, 0)


def landing(values, arrived, retain):
    layout = [1] * values.ndim
    layout[0] = values.shape[0]
    return jnp.where(retain.reshape(layout), arrived, values)


def spread_states(stacked, stacked_scales, chooser):
    data_parts, scale_parts = in_one_piece((stacked, stacked_scales), "dp", 2, 1, 3)
    data_back, scale_back = in_one_piece(
        (data_parts[:, chooser], scale_parts[:, chooser]), "dp", 1, 3, 4
    )
    return (data_back[:, 0], scale_back[:, 0])


def local(
    gradient,
    left_codes,
    left_scales,
    right_codes,
    right_scales,
    left_root_codes,
    left_root_scales,
    right_root_codes,
    right_root_scales,
    owner_plan,
):
    slot_count = gradient.shape[0]
    forward, backward, vacancy, retain = routing(owner_plan, slot_count)
    update, left_out, left_scale, right_out, right_scale = refresh(
        gradient,
        left_codes,
        left_scales,
        right_codes,
        right_scales,
        left_root_codes,
        left_root_scales,
        right_root_codes,
        right_root_scales,
    )
    stacked = jnp.stack([outgoing(left_out, vacancy), outgoing(right_out, vacancy)])
    stacked_scales = jnp.stack([outgoing(left_scale, vacancy), outgoing(right_scale, vacancy)])
    data_back, scale_back = spread_states(stacked, stacked_scales, forward)
    new_left = landing(left_out, data_back[0], retain)
    new_left_scale = landing(left_scale, scale_back[0], retain)
    new_right = landing(right_out, data_back[1], retain)
    new_right_scale = landing(right_scale, scale_back[1], retain)
    return (new_left, new_left_scale, new_right, new_right_scale, update)


def solution(mesh):
    placed = (
        P("dp", "mp", None),
        P("dp", "mp", None),
        P("dp", "mp"),
        P("dp", "mp", None),
        P("dp", "mp"),
        P("dp", "mp", None),
        P("dp", "mp"),
        P("dp", "mp", None),
        P("dp", "mp"),
        P(),
    )
    return jax.shard_map(
        local,
        mesh=mesh,
        in_specs=placed,
        out_specs=(
            P("dp", "mp", None),
            P("dp", "mp"),
            P("dp", "mp", None),
            P("dp", "mp"),
            P("dp", "mp", None),
        ),
        check_vma=False,
    )
```

profile of v0, /device:TPU:1, one launch (start us, length us, event | category | flops | bytes accessed | tf_op | source)
XLA Modules:
  0.0 179.1 jit_solution(12612929652434687628)
XLA Ops:
  8.8 2.3 %pad_maximum_fusion.1 = bf16[2,256,1025]{2,1,0:T(8,128)(2,1)} fusion(bf16[2,256,1]{2,1,0:T(8,128)(2,1)S(1)} %copy.68, bf16[2,256,1024]{2,1,0:T(8,128)(2,1)} %param.17), kind=kLoop, calls=%fused_computation.19 | loop fusion | flops 2099200 | bytes 2099200 | tf_op jit(solution)/shard_map/concatenate | solution.py:13
  13.9 50.6 %all-gather.3.cloned.1.call-done = bf16[2,1024,1024]{2,1,0:T(8,128)(2,1)} async-done(((bf16[2,256,1024]{2,1,0:T(8,128)(2,1)}), bf16[2,1024,1024]{2,1,0:T(8,128)(2,1)}) %all-gather.3.cloned.1.call-update) | async-done | bytes 4194320 | tf_op jit(solution)/shard_map/all_gather | solution.py:59
  64.5 4.5 %abs_reduce_fusion = (f32[2,256]{1,0:T(2,128)S(1)}, f32[2,256,1024]{2,1,0:T(8,128)S(1)}) fusion(bf16[2,1024,1024]{2,1,0:T(8,128)(2,1)} %all-gather.3.cloned.1.call-done, s32[]{:T(128)S(6)} %select_n.72, f32[2,256]{1,0:T(2,128)S(1)} %convert_element_type.78, bf16[2,256,1024]{2,1,0:T(8,128)(2,1)} %param.13), kind=kOutput, calls=%fused_computation.11 | convolution fusion | flops 1076887040 | bytes 8392708 | tf_op jit(solution)/shard_map/sji,sjk->sik/dot_general | solution.py:66
  69.0 1.5 abs_reduce_fusion.1
  72.1 2.3 %copy.60 = bf16[2,1,256,1025]{3,0,1,2:T(2,128)(2,1)} copy(bf16[2,1,256,1025]{3,2,1,0:T(8,128)(2,1)S(1)} %pad_maximum_fusion) | data formatting | bytes 2099200 | tf_op jit(solution)/shard_map/concatenate | solution.py:25
  74.4 10.7 %all-to-all-start = ((bf16[2,1,256,1025]{3,0,1,2:T(2,128)(2,1)}), bf16[2,1,256,1025]{3,0,1,2:T(2,128)(2,1)S(1)}, u32[]{:S(2)}, u32[]{:S(2)}) async-start(bf16[2,1,256,1025]{3,0,1,2:T(2,128)(2,1)} %copy.60), calls=%async_computation | async-start | bytes 2359296 | tf_op jit(solution)/shard_map/all_to_all | solution.py:27
  85.2 31.2 %all-to-all-done = bf16[2,1,256,1025]{3,0,1,2:T(2,128)(2,1)S(1)} async-done(((bf16[2,1,256,1025]{3,0,1,2:T(2,128)(2,1)}), bf16[2,1,256,1025]{3,0,1,2:T(2,128)(2,1)S(1)}, u32[]{:S(2)}, u32[]{:S(2)}) %all-to-all-start) | async-done | bytes 1049632 | tf_op jit(solution)/shard_map/all_to_all | solution.py:27
  116.5 2.1 %slice.38 = bf16[2,64,4,1024]{3,0,2,1:T(2,128)(2,1)} slice(bf16[2,64,4,1025]{3,0,2,1:T(2,128)(2,1)S(1)} %bitcast.37), slice={[0:2], [0:64], [0:4], [0:1024]} | slice | bytes 2097152 | tf_op jit(solution)/shard_map/slice | solution.py:32
  118.8 2.6 %copy.74 = bf16[2,64,4,1024]{3,2,1,0:T(4,128)(2,1)} copy(bf16[2,64,4,1024]{3,0,2,1:T(2,128)(2,1)} %slice.38) | data formatting | bytes 2097152
  121.5 2.7 %gather_fusion = bf16[64,2,4,1024]{3,2,1,0:T(4,128)(2,1)S(1)} fusion(bf16[2,64,4,1024]{3,2,1,0:T(4,128)(2,1)} %copy.74, s32[1024]{0:T(1024)S(1)} %pad_clamp_fusion), kind=kCustom, calls=%fused_computation | custom fusion | bytes 2097408 | tf_op jit(solution)/shard_map/gather | solution.py:122
  124.9 0.9 copy.65
  125.7 1.7 maximum_bitcast_fusion
  127.4 6.2 %all-to-all-start.1 = ((bf16[2,64,1,4,1025]{4,3,0,2,1:T(4,128)(2,1)}), bf16[2,64,1,4,1025]{4,3,0,2,1:T(4,128)(2,1)S(1)}, u32[]{:S(2)}, u32[]{:S(2)}) async-start(bf16[2,64,1,4,1025]{4,3,0,2,1:T(4,128)(2,1)} %maximum_bitcast_fusion), calls=%async_computation.1 | async-start | bytes 2359296 | tf_op jit(solution)/shard_map/all_to_all | solution.py:27
  134.2 1.3 compare_and_fusion
  135.5 1.6 multiply_reduce_fusion.1
  137.2 1.3 convert_reduce_fusion
  138.4 7.6 %multiply_reduce_fusion = (f32[2]{0:T(128)S(1)}, f32[2,256,1024]{2,1,0:T(8,128)}) fusion(bf16[2,1024,1025]{2,1,0:T(8,128)(2,1)} %all-gather.5.cloned.1.call-done, f32[2,1024]{1,0:T(2,128)S(1)} %convert_reduce_fusion, bf16[2,1024,1024]{2,1,0:T(8,128)(2,1)} %all-gather.3.cloned.1.call-done, bf16[2,256,1024]{2,1,0:T(8,128)(2,1)} %param.15, ...), kind=kOutput, calls=%fused_computation.7 | convolution fusion | flops 2156920832 | bytes 11544584 | tf_op jit(solution)/shard_map/sik,skj->sij/dot_general | solution.py:75
  146.0 7.4 %all-reduce = (f32[2]{0:T(128)S(1)}, f32[2]{0:T(128)S(1)}) all-reduce(f32[2]{0:T(128)S(1)} %get-tuple-element.25, f32[2]{0:T(128)S(1)} %multiply_reduce_fusion.1), channel_id=1, replica_groups=mesh['dp'=64,'mp'=4] {'mp'}, use_global_device_ids=true, to_apply=%region_8.9 | all-reduce | flops 4 | bytes 32 | tf_op jit(solution)/shard_map/psum | solution.py:78
  153.4 2.9 %multiply_convert_fusion.2 = bf16[2,256,1024]{2,1,0:T(8,128)(2,1)} fusion(f32[2,256,1024]{2,1,0:T(8,128)} %get-tuple-element.26, f32[2]{0:T(128)S(1)} %rsqrt_multiply_fusion), kind=kLoop, calls=%fused_computation.6 | loop fusion | flops 1048576 | bytes 3145736 | tf_op jit(solution)/shard_map/convert_element_type | solution.py:80
  156.2 8.7 %all-to-all-done.1 = bf16[2,64,1,4,1025]{4,3,0,2,1:T(4,128)(2,1)S(1)} async-done(((bf16[2,64,1,4,1025]{4,3,0,2,1:T(4,128)(2,1)}), bf16[2,64,1,4,1025]{4,3,0,2,1:T(4,128)(2,1)S(1)}, u32[]{:S(2)}, u32[]{:S(2)}) %all-to-all-start.1) | async-done | bytes 1049632 | tf_op jit(solution)/shard_map/all_to_all | solution.py:27
  164.9 0.9 copy.67
  165.9 1.1 slice_reduce_fusion
  167.0 1.5 fusion.16
  170.1 2.2 %broadcast_select_fusion = (bf16[2,256,1024]{2,1,0:T(8,128)(2,1)}, bf16[2,256,1024]{2,1,0:T(8,128)(2,1)}) fusion(pred[2]{0:T(512)(128)(4,1)S(1)} %compare_and_fusion, bf16[256,1024]{1,0:T(8,128)(2,1)S(1)} %bitcast.39, bf16[256,1024]{1,0:T(8,128)(2,1)S(1)} %bitcast.40, f32[2,256,1024]{2,1,0:T(8,128)S(1)} %copy-done.1, f32[2,256]{1,0:T(2,128)S(1)} %get-tuple-element.13, ...), kind=kLoop, calls=%fused_computation.23 | loop fusion | flops 3145728 | bytes 7344130 | tf_op jit(solution)/shard_map/jit(_where)/select_n | solution.py:116
  (51 shorter events, 7.2 us)
Async XLA Ops:
  7.2 57.3 %all-gather.3.cloned.1.call-start = ((), (), s32[]{:S(2)}) async-start(), calls=%async_computation.2 | async-start | bytes 5242880 | tf_op jit(solution)/shard_map/all_gather | solution.py:59
  7.9 3.3 %copy-start.8 = (s32[128]{0:T(128)S(1)}, s32[128]{0:T(128)}, u32[]{:S(2)}) copy-start(s32[128]{0:T(128)} %param.19) | copy-start | bytes 1540
  7.9 5.3 %copy-start.3 = (bf16[2,256]{1,0:T(2,128)(2,1)S(1)}, bf16[2,256]{1,0:T(2,128)(2,1)}, u32[]{:S(2)}) copy-start(bf16[2,256]{1,0:T(2,128)(2,1)} %param.12) | copy-start | bytes 3076
  7.9 5.3 %copy-start.4 = (bf16[2,256]{1,0:T(2,128)(2,1)S(1)}, bf16[2,256]{1,0:T(2,128)(2,1)}, u32[]{:S(2)}) copy-start(bf16[2,256]{1,0:T(2,128)(2,1)} %param.14) | copy-start | bytes 3076
  7.9 129.2 %all-gather.5.cloned.1.call-start = ((), (), s32[]{:S(2)}) async-start(), calls=%async_computation.3 | async-start | bytes 5898240 | tf_op jit(solution)/shard_map/all_gather | solution.py:16
  13.9 55.1 %copy-start.2 = (bf16[2,256,1024]{2,1,0:T(8,128)(2,1)S(1)}, bf16[2,256,1024]{2,1,0:T(8,128)(2,1)}, u32[]{:S(2)}) copy-start(bf16[2,256,1024]{2,1,0:T(8,128)(2,1)} %param.10) | copy-start | bytes 3145732
  64.5 4.5 %copy-start.6 = (bf16[2,1024,1024]{2,1,0:T(8,128)(2,1)S(1)}, bf16[2,1024,1024]{2,1,0:T(8,128)(2,1)}, u32[]{:S(2)}) copy-start(bf16[2,1024,1024]{2,1,0:T(8,128)(2,1)} %all-gather.3.cloned.1.call-done) | copy-start | bytes 12582916
  64.5 4.5 %copy-start.7 = (bf16[2,256,1024]{2,1,0:T(8,128)(2,1)S(1)}, bf16[2,256,1024]{2,1,0:T(8,128)(2,1)}, u32[]{:S(2)}) copy-start(bf16[2,256,1024]{2,1,0:T(8,128)(2,1)} %param.11) | copy-start | bytes 3145732
  70.5 1.4 copy-start
  74.4 42.1 %all-to-all-start = ((bf16[2,1,256,1025]{3,0,1,2:T(2,128)(2,1)}), bf16[2,1,256,1025]{3,0,1,2:T(2,128)(2,1)S(1)}, u32[]{:S(2)}, u32[]{:S(2)}) async-start(bf16[2,1,256,1025]{3,0,1,2:T(2,128)(2,1)} %copy.60), calls=%async_computation | async-start | bytes 2359296 | tf_op jit(solution)/shard_map/all_to_all | solution.py:27
  125.7 7.9 %copy-start.5 = (bf16[2,256]{1,0:T(2,128)(2,1)S(1)}, bf16[2,256]{1,0:T(2,128)(2,1)}, u32[]{:S(2)}) copy-start(bf16[2,256]{1,0:T(2,128)(2,1)} %param.16) | copy-start | bytes 3076
  127.4 37.6 %all-to-all-start.1 = ((bf16[2,64,1,4,1025]{4,3,0,2,1:T(4,128)(2,1)}), bf16[2,64,1,4,1025]{4,3,0,2,1:T(4,128)(2,1)S(1)}, u32[]{:S(2)}, u32[]{:S(2)}) async-start(bf16[2,64,1,4,1025]{4,3,0,2,1:T(4,128)(2,1)} %maximum_bitcast_fusion), calls=%async_computation.1 | async-start | bytes 2359296 | tf_op jit(solution)/shard_map/all_to_all | solution.py:27
  168.5 1.6 copy-start.1
Sparse Core Ops, SparseCore 0:
  9.8 54.5 all-gather.2
  66.3 55.5 all-gather.4
where the time goes:
time: 180 us; the launch traced here: 179 us
  waiting for transfers between devices  91.2 us (51%)
  local copies, waits for them, and re-layouts  17.7 us (10%)
  starting transfers between devices  17 us (9%)
  between operations  16.3 us (9%)
  other arithmetic  16 us (9%)
  matrix products  13.6 us (8%)
  blocking collectives  7.38 us (4%)
    all_gather x1, waiting for transfers between devices, refresh(): gathered = lax.all_gather(gradient, 'mp', axis=1, tiled=True)  50.6 us
    all_to_all x2, waiting for transfers between devices, in_one_piece(): lax.all_to_all(both, axis, split_axis=split_dim, concat_axis=concat_dim,...  39.9 us
    all_to_all x2, starting transfers between devices, in_one_piece(): lax.all_to_all(both, axis, split_axis=split_dim, concat_axis=concat_dim,...  16.9 us
    dot_general x1, matrix products, refresh(): jnp.einsum('sik,skj->sij', lifted, root_piece, preferred_element_type=jnp...  7.56 us
    psum x1, blocking collectives, refresh(): grad_total, dir_total = lax.psum((grad_square, dir_square), 'mp')  7.38 us
    dot_general x1, matrix products, refresh(): jnp.einsum('sji,sjk->sik', columns, gathered, preferred_element_type=jnp....  4.49 us
    unnamed x21, local copies, waits for them, and re-layouts  4.16 us
  transfers between devices with their start and end apart: 4, of which 3 were waited for; matrix products, arithmetic and copies ran while one was open for 22% of the time, Pallas kernels for 0%

commit v1 on v0

--- a/solution.py
+++ b/solution.py
@@ -56,7 +56,9 @@
     right_root_codes,
     right_root_scales,
 ):
-    gathered = lax.all_gather(gradient, "mp", axis=1, tiled=True)
+    gathered = jnp.concatenate(
+        lax.all_to_all(jnp.stack([gradient] * lax.axis_size("mp")), "mp", 0, 0), axis=1
+    )
     height = gradient.shape[1]
     offset = lax.axis_index("mp") * height
     left_new = DECAY * dequantize(left_codes, left_scales) + jnp.einsum(

time: 180 us -> 209 us (1.16)
  starting transfers between devices: 17 us -> 32.1 us
  waiting for transfers between devices: 91.2 us -> 106 us
  local copies, waits for them, and re-layouts: 17.7 us -> 21.6 us
  matrix products: 13.6 us -> 10.8 us
    all_to_all x0 -> x1, waiting for transfers between devices: none -> 65.6 us  [refresh(): lax.all_to_all(jnp.stack([gradient] * lax.axis_size('mp')), 'mp', 0, 0)]
    all_gather x1 -> x0, waiting for transfers between devices: 50.6 us -> none  [refresh(): gathered = lax.all_gather(gradient, 'mp', axis=1, tiled=True)]
    all_to_all x2, starting transfers between devices: 16.9 us -> 27 us  [in_one_piece(): lax.all_to_all(both, axis, split_axis=split_dim, concat_axis=concat_dim,...]
    all_to_all x0 -> x1, starting transfers between devices: none -> 5.14 us  [refresh(): lax.all_to_all(jnp.stack([gradient] * lax.axis_size('mp')), 'mp', 0, 0)]
    another operation x0 -> x1, local copies, waits for them, and re-layouts: none -> 3.76 us  [refresh(): jnp.stack([gradient] * lax.axis_size('mp'))]
    dot_general x1, matrix products: 4.49 us -> 1.58 us  [refresh(): jnp.einsum('sji,sjk->sik', columns, gathered, preferred_element_type=jnp....]
    reshape x0 -> x1, local copies, waits for them, and re-layouts: none -> 2.74 us  [refresh(): jnp.concatenate(lax.all_to_all(jnp.stack([gradient] * lax.axis_size('mp')...]
  transfers between devices with their start and end apart: 4 -> 4, of which waited for: 3 -> 3; matrix products, arithmetic and copies ran while one was open for 22% -> 17% of each run, Pallas kernels for 0% -> 0%
where the time goes in v1:
time: 209 us; the launch traced here: 208 us
  waiting for transfers between devices  106 us (51%)
  starting transfers between devices  32.1 us (15%)
  local copies, waits for them, and re-layouts  21.6 us (10%)
  between operations  16.3 us (8%)
  other arithmetic  14.2 us (7%)
  matrix products  10.8 us (5%)
  blocking collectives  6.76 us (3%)
    all_to_all x1, waiting for transfers between devices, refresh(): lax.all_to_all(jnp.stack([gradient] * lax.axis_size('mp')), 'mp', 0, 0)  65.6 us
    all_to_all x2, waiting for transfers between devices, in_one_piece(): lax.all_to_all(both, axis, split_axis=split_dim, concat_axis=concat_dim,...  40.5 us
    all_to_all x2, starting transfers between devices, in_one_piece(): lax.all_to_all(both, axis, split_axis=split_dim, concat_axis=concat_dim,...  27 us
    dot_general x1, matrix products, refresh(): jnp.einsum('sik,skj->sij', lifted, root_piece, preferred_element_type=jnp...  7.58 us
    psum x1, blocking collectives, refresh(): grad_total, dir_total = lax.psum((grad_square, dir_square), 'mp')  6.76 us
    all_to_all x1, starting transfers between devices, refresh(): lax.all_to_all(jnp.stack([gradient] * lax.axis_size('mp')), 'mp', 0, 0)  5.14 us
  transfers between devices with their start and end apart: 4, of which 3 were waited for; matrix products, arithmetic and copies ran while one was open for 17% of the time, Pallas kernels for 0%

profile of v1, /device:TPU:1, one launch (start us, length us, event | category | flops | bytes accessed | tf_op | source)
XLA Modules:
  0.0 207.9 jit_solution(6381128374285487603)
XLA Ops:
  7.2 3.8 %stack.25 = bf16[4,2,256,1024]{3,2,1,0:T(8,128)(2,1)} broadcast(bf16[2,256,1024]{2,1,0:T(8,128)(2,1)} %param.10), dimensions={1,2,3} | broadcast | bytes 5242880 | tf_op jit(solution)/shard_map/stack | solution.py:60
  10.9 5.1 %all-to-all-start = ((bf16[4,2,256,1024]{3,2,1,0:T(8,128)(2,1)}), bf16[4,2,256,1024]{3,2,1,0:T(8,128)(2,1)}, u32[]{:S(2)}, u32[]{:S(2)}) async-start(bf16[4,2,256,1024]{3,2,1,0:T(8,128)(2,1)} %stack.25), calls=%async_computation | async-start | bytes 8388608 | tf_op jit(solution)/shard_map/all_to_all | solution.py:60
  16.3 1.1 pad_maximum_fusion.1
  20.2 65.6 %all-to-all-done = bf16[4,2,256,1024]{3,2,1,0:T(8,128)(2,1)} async-done(((bf16[4,2,256,1024]{3,2,1,0:T(8,128)(2,1)}), bf16[4,2,256,1024]{3,2,1,0:T(8,128)(2,1)}, u32[]{:S(2)}, u32[]{:S(2)}) %all-to-all-start) | async-done | bytes 4194336 | tf_op jit(solution)/shard_map/all_to_all | solution.py:60
  85.7 2.7 %copy.60 = bf16[2,4,256,1024]{3,2,1,0:T(8,128)(2,1)S(1)} copy(bf16[2,4,256,1024]{3,2,0,1:T(8,128)(2,1)} %bitcast) | data formatting | bytes 8388608 | tf_op jit(solution)/shard_map/reshape | solution.py:59
  88.5 1.6 abs_reduce_fusion
  91.6 1.6 abs_reduce_fusion.1
  94.1 2.3 %copy.63 = bf16[2,1,256,1025]{3,0,1,2:T(2,128)(2,1)} copy(bf16[2,1,256,1025]{3,2,1,0:T(8,128)(2,1)S(1)} %pad_maximum_fusion) | data formatting | bytes 2099200 | tf_op jit(solution)/shard_map/concatenate | solution.py:25
  96.4 20.8 %all-to-all-start.1 = ((bf16[2,1,256,1025]{3,0,1,2:T(2,128)(2,1)}), bf16[2,1,256,1025]{3,0,1,2:T(2,128)(2,1)S(1)}, u32[]{:S(2)}, u32[]{:S(2)}) async-start(bf16[2,1,256,1025]{3,0,1,2:T(2,128)(2,1)} %copy.63), calls=%async_computation.1 | async-start | bytes 2359296 | tf_op jit(solution)/shard_map/all_to_all | solution.py:27
  117.3 31.2 %all-to-all-done.1 = bf16[2,1,256,1025]{3,0,1,2:T(2,128)(2,1)S(1)} async-done(((bf16[2,1,256,1025]{3,0,1,2:T(2,128)(2,1)}), bf16[2,1,256,1025]{3,0,1,2:T(2,128)(2,1)S(1)}, u32[]{:S(2)}, u32[]{:S(2)}) %all-to-all-start.1) | async-done | bytes 1049632 | tf_op jit(solution)/shard_map/all_to_all | solution.py:27
  148.5 1.1 slice.38
  149.8 1.4 copy.77
  151.4 2.7 %gather_fusion = bf16[64,2,4,1024]{3,2,1,0:T(4,128)(2,1)S(1)} fusion(bf16[2,64,4,1024]{3,2,1,0:T(4,128)(2,1)} %copy.77, s32[1024]{0:T(1024)S(1)} %pad_clamp_fusion), kind=kCustom, calls=%fused_computation | custom fusion | bytes 2097408 | tf_op jit(solution)/shard_map/gather | solution.py:124
  155.6 1.6 maximum_bitcast_fusion
  157.3 6.2 %all-to-all-start.2 = ((bf16[2,64,1,4,1025]{4,3,0,2,1:T(4,128)(2,1)}), bf16[2,64,1,4,1025]{4,3,0,2,1:T(4,128)(2,1)S(1)}, u32[]{:S(2)}, u32[]{:S(2)}) async-start(bf16[2,64,1,4,1025]{4,3,0,2,1:T(4,128)(2,1)} %maximum_bitcast_fusion), calls=%async_computation.2 | async-start | bytes 2359296 | tf_op jit(solution)/shard_map/all_to_all | solution.py:27
  164.1 1.3 compare_and_fusion
  165.4 1.6 multiply_reduce_fusion.1
  167.0 1.3 convert_reduce_fusion
  168.3 7.6 %multiply_reduce_fusion = (f32[2]{0:T(128)S(1)}, f32[2,256,1024]{2,1,0:T(8,128)}) fusion(bf16[2,1024,1025]{2,1,0:T(8,128)(2,1)} %all-gather.2.cloned.1.call-done, f32[2,1024]{1,0:T(2,128)S(1)} %convert_reduce_fusion, bf16[2,1024,1024]{2,1,0:T(8,128)(2,1)} %bitcast.43, bf16[2,256,1024]{2,1,0:T(8,128)(2,1)} %param.15, f32[2,256]{1,0:T(2,128)S(1)} %convert_element_type.83), kind=kOutput, calls=%fused_computation.7 | convolution fusion | flops 2156920832 | bytes 11544584 | tf_op jit(solution)/shard_map/sik,skj->sij/dot_general | solution.py:77
  175.9 6.8 %all-reduce = (f32[2]{0:T(128)S(1)}, f32[2]{0:T(128)S(1)}) all-reduce(f32[2]{0:T(128)S(1)} %get-tuple-element.25, f32[2]{0:T(128)S(1)} %multiply_reduce_fusion.1), channel_id=1, replica_groups=mesh['dp'=64,'mp'=4] {'mp'}, use_global_device_ids=true, to_apply=%region_8.9 | all-reduce | flops 4 | bytes 32 | tf_op jit(solution)/shard_map/psum | solution.py:80
  182.7 2.9 %multiply_convert_fusion.2 = bf16[2,256,1024]{2,1,0:T(8,128)(2,1)} fusion(f32[2,256,1024]{2,1,0:T(8,128)} %get-tuple-element.26, f32[2]{0:T(128)S(1)} %rsqrt_multiply_fusion), kind=kLoop, calls=%fused_computation.6 | loop fusion | flops 1048576 | bytes 3145736 | tf_op jit(solution)/shard_map/convert_element_type | solution.py:82
  185.5 9.3 %all-to-all-done.2 = bf16[2,64,1,4,1025]{4,3,0,2,1:T(4,128)(2,1)S(1)} async-done(((bf16[2,64,1,4,1025]{4,3,0,2,1:T(4,128)(2,1)}), bf16[2,64,1,4,1025]{4,3,0,2,1:T(4,128)(2,1)S(1)}, u32[]{:S(2)}, u32[]{:S(2)}) %all-to-all-start.2) | async-done | bytes 1049632 | tf_op jit(solution)/shard_map/all_to_all | solution.py:27
  196.9 1.5 fusion.16
  199.4 1.7 broadcast_select_fusion
  (54 shorter events, 8.9 us)
Async XLA Ops:
  10.9 5.2 %copy-start.3 = (bf16[2,256]{1,0:T(2,128)(2,1)S(1)}, bf16[2,256]{1,0:T(2,128)(2,1)}, u32[]{:S(2)}) copy-start(bf16[2,256]{1,0:T(2,128)(2,1)} %param.18) | copy-start | bytes 3076
  10.9 5.4 %copy-start.2 = (bf16[2,256,1024]{2,1,0:T(8,128)(2,1)S(1)}, bf16[2,256,1024]{2,1,0:T(8,128)(2,1)}, u32[]{:S(2)}) copy-start(bf16[2,256,1024]{2,1,0:T(8,128)(2,1)} %param.17) | copy-start | bytes 3145732
  10.9 74.8 %all-to-all-start = ((bf16[4,2,256,1024]{3,2,1,0:T(8,128)(2,1)}), bf16[4,2,256,1024]{3,2,1,0:T(8,128)(2,1)}, u32[]{:S(2)}, u32[]{:S(2)}) async-start(bf16[4,2,256,1024]{3,2,1,0:T(8,128)(2,1)} %stack.25), calls=%async_computation | async-start | bytes 8388608 | tf_op jit(solution)/shard_map/all_to_all | solution.py:60
  16.1 1.4 copy-start.9
  16.1 3.4 %copy-start.4 = (bf16[2,256]{1,0:T(2,128)(2,1)S(1)}, bf16[2,256]{1,0:T(2,128)(2,1)}, u32[]{:S(2)}) copy-start(bf16[2,256]{1,0:T(2,128)(2,1)} %param.14) | copy-start | bytes 3076
  16.1 3.4 %copy-start.5 = (bf16[2,256]{1,0:T(2,128)(2,1)S(1)}, bf16[2,256]{1,0:T(2,128)(2,1)}, u32[]{:S(2)}) copy-start(bf16[2,256]{1,0:T(2,128)(2,1)} %param.12) | copy-start | bytes 3076
  16.1 150.9 %all-gather.2.cloned.1.call-start = ((), (), s32[]{:S(2)}) async-start(), calls=%async_computation.3 | async-start | bytes 5898240 | tf_op jit(solution)/shard_map/all_gather | solution.py:16
  85.7 2.8 %copy-start.7 = (bf16[2,256,1024]{2,1,0:T(8,128)(2,1)S(1)}, bf16[2,256,1024]{2,1,0:T(8,128)(2,1)}, u32[]{:S(2)}) copy-start(bf16[2,256,1024]{2,1,0:T(8,128)(2,1)} %param.13) | copy-start | bytes 3145732
  88.5 2.1 %copy-start.1 = (bf16[2,4,256,1024]{3,2,1,0:T(8,128)(2,1)}, bf16[2,4,256,1024]{3,2,1,0:T(8,128)(2,1)S(1)}, u32[]{:S(2)}) copy-start(bf16[2,4,256,1024]{3,2,1,0:T(8,128)(2,1)S(1)} %copy.60) | copy-start | bytes 12582916
  88.5 2.1 %copy-start = (bf16[2,256,1024]{2,1,0:T(8,128)(2,1)S(1)}, bf16[2,256,1024]{2,1,0:T(8,128)(2,1)}, u32[]{:S(2)}) copy-start(bf16[2,256,1024]{2,1,0:T(8,128)(2,1)} %param.10) | copy-start | bytes 3145732
  88.5 3.1 %copy-start.8 = (bf16[2,256,1024]{2,1,0:T(8,128)(2,1)S(1)}, bf16[2,256,1024]{2,1,0:T(8,128)(2,1)}, u32[]{:S(2)}) copy-start(bf16[2,256,1024]{2,1,0:T(8,128)(2,1)} %param.11) | copy-start | bytes 3145732
  96.4 52.1 %all-to-all-start.1 = ((bf16[2,1,256,1025]{3,0,1,2:T(2,128)(2,1)}), bf16[2,1,256,1025]{3,0,1,2:T(2,128)(2,1)S(1)}, u32[]{:S(2)}, u32[]{:S(2)}) async-start(bf16[2,1,256,1025]{3,0,1,2:T(2,128)(2,1)} %copy.63), calls=%async_computation.1 | async-start | bytes 2359296 | tf_op jit(solution)/shard_map/all_to_all | solution.py:27
  155.6 7.8 %copy-start.6 = (bf16[2,256]{1,0:T(2,128)(2,1)S(1)}, bf16[2,256]{1,0:T(2,128)(2,1)}, u32[]{:S(2)}) copy-start(bf16[2,256]{1,0:T(2,128)(2,1)} %param.16) | copy-start | bytes 3076
  157.3 37.6 %all-to-all-start.2 = ((bf16[2,64,1,4,1025]{4,3,0,2,1:T(4,128)(2,1)}), bf16[2,64,1,4,1025]{4,3,0,2,1:T(4,128)(2,1)S(1)}, u32[]{:S(2)}, u32[]{:S(2)}) async-start(bf16[2,64,1,4,1025]{4,3,0,2,1:T(4,128)(2,1)} %maximum_bitcast_fusion), calls=%async_computation.2 | async-start | bytes 2359296 | tf_op jit(solution)/shard_map/all_to_all | solution.py:27
Sparse Core Ops, SparseCore 0:
  18.7 85.3 all-gather.1
